TPU v7x, 256 devices: a whole 4x4x8 slice. The times are simulated.
256 devices in a mesh: wide: 32 (over z_hi, x, y), narrow: 8 (over z_lo, core).
Axes of the slice: x: 4, y: 4, z: 8 (z_hi: 2, z_lo: 4; z = z_hi * 4 + z_lo), core: 2. Of those that a mesh axis runs over, the one named last changes fastest.
Arguments:
- latent: float32 [2, 256, 512, 512], P(None, 'wide', 'narrow'), may hold values from -6 to 6
- context: bfloat16 [2, 128, 256, 256], P(None, 'wide', 'narrow'), may hold values from -6 to 6
- conv_weight: bfloat16 [3, 3, 256, 512], replicated, may hold values from -0.125 to 0.125
- window_qkv: bfloat16 [512, 1536], replicated, may hold values from -0.25 to 0.25
- window_out: bfloat16 [512, 512], replicated, may hold values from -0.25 to 0.25
- window_bias: float32 [16, 15, 15], replicated, may hold values from -9 to 320
- grid_qkv: bfloat16 [512, 1536], replicated, may hold values from -0.25 to 0.25
- grid_out: bfloat16 [512, 512], replicated, may hold values from -0.25 to 0.25
- grid_bias: float32 [16, 15, 15], replicated, may hold values from -9 to 320
- mlp_gain: float32 [512], replicated, may hold values from 0.1 to 1.9
- mlp_in: bfloat16 [512, 2048], replicated, may hold values from -0.25 to 0.25
- mlp_out: bfloat16 [2048, 512], replicated, may hold values from -0.125 to 0.125
Outputs:
- forecast: float32 [2, 256, 512, 512], P(None, 'wide', 'narrow')
All inputs are finite; a program needn't handle non-finite values.
Results may differ from a plain program's by a relative error of at most 0.0055.
Values may be sent and summed in bfloat16 or wider, within the bound.
A program may use at most 128 MiB of HBM per device.

v0:
```python
import math

import jax
import jax.numpy as jnp
from jax import lax
from jax.experimental import pallas as pl
from jax.experimental.pallas import tpu as pltpu
from jax.sharding import PartitionSpec as P

MESH = pl.DeviceIdType.MESH
F32 = jnp.float32
BF16 = jnp.bfloat16
NORM_EPS = 1e-05
HEAD = 32
WIN = 8
CELLS = WIN * WIN
LOG2E = 1.4426950408889634
CTX_COLS = 48


def iota(shape, dim):
    return lax.broadcasted_iota(jnp.int32, shape, dim)


def dot_nn(a, b):
    return jnp.dot(a, b, preferred_element_type=F32)


def dot_nt(a, b):
    return lax.dot_general(a, b, (((1,), (1,)), ((), ())), preferred_element_type=F32)


def layer_norm(values):
    center = values - jnp.mean(values, axis=-1, keepdims=True)
    spread = jnp.mean(center * center, axis=-1, keepdims=True)
    return center * lax.rsqrt(spread + NORM_EPS)


def identity(size):
    return jnp.where(iota((size, size), 0) == iota((size, size), 1), 1.0, 0.0).astype(BF16)


def fill_upsampler(up_ref):
    rows, depth = up_ref.shape
    lane = iota((1, depth), 1)
    coarse_row = jnp.zeros((1, depth), jnp.int32)
    for step in range(1, depth // CTX_COLS):
        coarse_row = coarse_row + jnp.where(lane >= step * CTX_COLS, 1, 0)
    coarse_col = lane - coarse_row * CTX_COLS
    block = 64
    for start in range(0, rows, block):
        fine_row = start // 64
        row_centre = fine_row // 2 + 1
        row_other = fine_row // 2 + (2 if fine_row % 2 else 0)
        row_weight = jnp.where(coarse_row == row_centre, 0.75, 0.0) + jnp.where(
            coarse_row == row_other, 0.25, 0.0
        )
        fine_col = iota((block, depth), 0)
        col_centre = (fine_col >> 1) + 8
        col_other = col_centre + 2 * (fine_col & 1) - 1
        col_weight = jnp.where(coarse_col == col_centre, 0.75, 0.0) + jnp.where(
            coarse_col == col_other, 0.25, 0.0
        )
        up_ref[pl.ds(start, block), :] = (row_weight * col_weight).astype(BF16)


def fill_bias(table, which, spread_ref, step_ref, bias_ref):
    pick = jnp.where(iota((16, 1024), 0) == (iota((16, 1024), 1) >> 6), 1.0, 0.0)
    spread_ref[...] = (
        jnp.dot(table, pick, preferred_element_type=F32, precision=lax.Precision.HIGHEST) * LOG2E
    )
    col_step = (iota((8, 1024), 1) & 7) - iota((8, 1024), 0) + 7

    def one_row_step(a, carry):
        rows = spread_ref[pl.ds(pl.multiple_of(a * 16, 16), 16), :]
        total = jnp.zeros((8, 1024), F32)
        for j in range(15):
            total = jnp.where(col_step == j, jnp.broadcast_to(rows[j : j + 1], (8, 1024)), total)
        step_ref[a] = total
        return carry

    lax.fori_loop(0, 15, one_row_step, 0)
    query_row = (iota((8, 1024), 1) >> 3) & 7

    def one_key_row(rq, carry):
        total = jnp.zeros((8, 1024), F32)
        for rp in range(8):
            total = jnp.where(query_row == rp, step_ref[rp - rq + 7], total)
        for block in range(4):
            bias_ref[which, block, pl.ds(pl.multiple_of(rq * 8, 8), 8), :] = total[
                :, block * 256 : (block + 1) * 256
            ]
        return carry

    lax.fori_loop(0, 8, one_key_row, 0)


def attend(x, qkv_ref, value_ref, bias_ref, which):
    width = x.shape[1]
    queries = dot_nn(x, qkv_ref[:, 0:width]).astype(BF16)
    keys = dot_nn(x, qkv_ref[:, width : 2 * width]).astype(BF16)
    values = dot_nt(value_ref[which], x).astype(BF16)
    head_of_lane = iota((CELLS, 128), 1) >> 5
    head_masks = [jnp.where(head_of_lane == h, 1.0, 0.0).astype(BF16) for h in range(4)]
    group_of_lane = iota((128, 256), 1) >> 6
    group_masks = [jnp.where(group_of_lane == g, 1.0, 0.0).astype(BF16) for g in range(4)]
    low = iota((HEAD, 128), 1) < 64
    outs = []
    for block in range(width // 128):
        lanes = slice(block * 128, (block + 1) * 128)
        bias = bias_ref[which, block]
        weights = []
        for g in range(4):
            rows = slice(g * CELLS, (g + 1) * CELLS)
            query = queries[rows, lanes]
            spread = jnp.concatenate([query * mask for mask in head_masks], axis=0)
            scores = dot_nt(keys[rows, lanes], spread) * (LOG2E * HEAD**-0.5) + bias
            lifted = jnp.exp2(scores - jnp.max(scores, axis=0, keepdims=True))
            inverse = 1.0 / jnp.sum(lifted, axis=0, keepdims=True)
            weights.append((lifted * inverse).astype(BF16))
        weight = jnp.concatenate(weights, axis=0)
        value = values[lanes]
        stacked = jnp.concatenate([value * mask for mask in group_masks], axis=0)
        blended = dot_nn(stacked, weight)
        for h in range(4):
            picked = []
            for pair in range(2):
                parts = []
                for g in (2 * pair, 2 * pair + 1):
                    parts.append(
                        blended[
                            g * 128 + h * HEAD : g * 128 + (h + 1) * HEAD,
                            (h // 2) * 128 : (h // 2 + 1) * 128,
                        ]
                    )
                first, second = parts
                if h % 2 == 0:
                    picked.append(jnp.where(low, first, pltpu.roll(second, 64, 1)))
                else:
                    picked.append(jnp.where(low, pltpu.roll(first, 64, 1), second))
            outs.append(jnp.concatenate(picked, axis=1).astype(BF16))
    turned = jnp.concatenate(outs, axis=0)
    return dot_nt(identity(4 * CELLS), turned).astype(BF16)


def block_kernel(
    latent_ref,
    context_ref,
    conv_hbm,
    window_qkv_hbm,
    window_out_hbm,
    grid_qkv_hbm,
    grid_out_hbm,
    mlp_in_hbm,
    mlp_out_hbm,
    table_ref,
    gain_ref,
    out_ref,
    res,
    halo,
    conv_w,
    window_qkv,
    window_out,
    grid_qkv,
    grid_out,
    mlp_in,
    mlp_out,
    value_t,
    up,
    bias,
    spread,
    steps,
    perm,
    sent,
    received,
    answers,
    returned,
    grouped,
    heads_buf,
    load_sem,
    halo_send,
    halo_recv,
    there_send,
    there_recv,
    back_send,
    back_recv,
    out_sem,
):
    wide = lax.axis_index("wide")
    narrow = lax.axis_index("narrow")
    wide_count = lax.axis_size("wide")
    narrow_count = lax.axis_size("narrow")
    planes = wide_count // WIN
    plane = lax.rem(wide, planes)
    my_row = wide // planes
    me = my_row * WIN + narrow

    def device(place):
        return ((place // WIN) * planes + plane, lax.rem(place, WIN))

    loads = [
        pltpu.make_async_copy(source, target, load_sem.at[i])
        for i, (source, target) in enumerate(
            (
                (conv_hbm, conv_w),
                (latent_ref, res),
                (window_qkv_hbm, window_qkv),
                (window_out_hbm, window_out),
                (grid_qkv_hbm, grid_qkv),
                (grid_out_hbm, grid_out),
                (mlp_in_hbm, mlp_in),
                (mlp_out_hbm, mlp_out),
            )
        )
    ]
    own = pltpu.make_async_copy(context_ref, halo.at[:, pl.ds(2, 4), pl.ds(16, 32), :], halo_recv)
    own.start()

    barrier = pltpu.get_barrier_semaphore()

    def greet(i, carry):
        pl.semaphore_signal(
            barrier, inc=1, device_id=device(lax.rem(me + i, CELLS)), device_id_type=MESH
        )
        return carry

    around = []
    for dw in (-1, 0, 1):
        for dn in (-1, 0, 1):
            if dw or dn:
                around.append((dw, dn))

    def neighbour(dw, dn):
        return (
            lax.rem(wide + dw + wide_count, wide_count),
            lax.rem(narrow + dn + narrow_count, narrow_count),
        )

    for dw, dn in around:
        if dw:
            pl.semaphore_signal(barrier, inc=1, device_id=neighbour(dw, dn), device_id_type=MESH)
    lax.fori_loop(1, CELLS, greet, 0)
    for load in loads:
        load.start()
    pl.semaphore_wait(barrier, CELLS - 1 + 6)

    sends = []
    row_cut = {-1: (0, 2, 6), 0: (0, 4, 2), 1: (2, 2, 0)}
    col_cut = {-1: (0, 16, 48), 0: (0, 32, 16), 1: (16, 16, 0)}
    for dw, dn in around:
        row_from, rows, row_to = row_cut[dw]
        col_from, cols, col_to = col_cut[dn]
        copy = pltpu.make_async_remote_copy(
            src_ref=context_ref.at[:, pl.ds(row_from, rows), pl.ds(col_from, cols), :],
            dst_ref=halo.at[:, pl.ds(row_to, rows), pl.ds(col_to, cols), :],
            send_sem=halo_send.at[len(sends)],
            recv_sem=halo_recv,
            device_id=neighbour(dw, dn),
            device_id_type=MESH,
        )
        copy.start()
        sends.append(copy)

    fill_upsampler(up)
    out_row = iota((256, 256), 0)
    in_row = iota((256, 256), 1)
    perm[0] = jnp.where(
        in_row == (out_row & 15) * 16 + (out_row >> 7) * 8 + ((out_row >> 4) & 7), 1.0, 0.0
    ).astype(BF16)
    perm[1] = jnp.where(
        out_row == (in_row & 15) * 16 + (in_row >> 7) * 8 + ((in_row >> 4) & 7), 1.0, 0.0
    ).astype(BF16)
    fill_bias(table_ref[0], 0, spread, steps, bias)
    fill_bias(table_ref[1], 1, spread, steps, bias)
    width = window_out.shape[0]
    loads[2].wait()
    value_t[0] = dot_nt(identity(width), window_qkv[:, 2 * width :]).astype(BF16)
    loads[4].wait()
    value_t[1] = dot_nt(identity(width), grid_qkv[:, 2 * width :]).astype(BF16)

    pltpu.make_async_copy(halo, halo, halo_recv).wait()
    loads[0].wait()
    loads[1].wait()
    depth = context_ref.shape[3]
    half_rows, half_cols = context_ref.shape[1], context_ref.shape[2]
    batch = latent_ref.shape[0]

    def convolve(b, carry):
        widened = halo[b].astype(F32)[:, 8:56, :]
        shape = (8, CTX_COLS, depth)
        row_place = wide * half_rows - 2 + iota(shape, 0)
        col_place = narrow * half_cols - 8 + iota(shape, 1)
        inside = (
            (row_place >= 0)
            & (row_place < wide_count * half_rows)
            & (col_place >= 0)
            & (col_place < narrow_count * half_cols)
        )
        widened = jnp.where(inside, widened, 0.0).astype(BF16)
        rows = 6 * CTX_COLS
        tall = jnp.concatenate([widened[i : i + 6].reshape(rows, depth) for i in range(3)], axis=1)
        left, centre, right = [
            dot_nn(tall, conv_w[:, dl].reshape(3 * depth, width)) for dl in range(3)
        ]
        total = centre + pltpu.roll(left, 1, 0) + pltpu.roll(right, rows - 1, 0)
        shape = (6, CTX_COLS, width)
        row_place = wide * half_rows - 1 + iota(shape, 0)
        col_place = narrow * half_cols - 8 + iota(shape, 1)
        inside = (
            (row_place >= 0)
            & (row_place < wide_count * half_rows)
            & (col_place >= 0)
            & (col_place < narrow_count * half_cols)
        )
        features = jnp.where(inside.reshape(rows, width), total, 0.0).astype(BF16)
        res[b] = res[b] + dot_nn(up[...], features).reshape(res.shape[1:])
        return carry

    lax.fori_loop(0, batch, convolve, 0)
    loads[3].wait()

    def windows(step, carry):
        b, half = step // 2, lax.rem(step, 2)
        places = [lax.rem(narrow + half * 4 + i, WIN) for i in range(4)]
        before = jnp.concatenate([res[b, :, place].reshape(CELLS, width) for place in places], axis=0)
        normed = layer_norm(before).astype(BF16)
        heads = attend(normed, window_qkv, value_t, bias, 0)
        after = before + dot_nn(heads, window_out[...])
        normed = layer_norm(after).reshape(4, WIN, WIN, width)
        for i, place in enumerate(places):
            res[b, :, place] = after[i * CELLS : (i + 1) * CELLS].reshape(WIN, WIN, width)
            sent[b, place] = jnp.concatenate(
                [normed[i, :, :, : width // 2], normed[i, :, :, width // 2 :]], axis=1
            ).astype(BF16)

        def post(i, carry):
            place = lax.rem(narrow + half * 4 + i // WIN, WIN)
            row = lax.rem(my_row + lax.rem(i, WIN), WIN)
            target = row * WIN + place

            @pl.when(target == me)
            def _():
                pltpu.make_async_copy(
                    sent.at[b, place, row], received.at[b, me], there_recv.at[b]
                ).start()

            @pl.when(target != me)
            def _():
                pltpu.make_async_remote_copy(
                    src_ref=sent.at[b, place, row],
                    dst_ref=received.at[b, me],
                    send_sem=there_send.at[b],
                    recv_sem=there_recv.at[b],
                    device_id=device(target),
                    device_id_type=MESH,
                ).start()

            return carry

        lax.fori_loop(0, 4 * WIN, post, 0)
        return carry

    lax.fori_loop(0, 2 * batch, windows, 0)

    def grid(b, carry):
        pltpu.make_async_copy(received.at[b], received.at[b], there_recv.at[b]).wait()
        half_width = width // 2
        for chunk in range(4):
            rows = received[b, chunk * 16 : (chunk + 1) * 16].reshape(256, half_width)
            turned = dot_nn(perm[0], rows).astype(BF16)
            for half in range(2):
                grouped[:, chunk * 16 : (chunk + 1) * 16, half * half_width : (half + 1) * half_width] = (
                    turned[half * 128 : (half + 1) * 128].reshape(WIN, 16, half_width)
                )

        def groups(part, carry):
            start = part * 4
            x = grouped[pl.ds(start, 4)].reshape(4 * CELLS, width)
            heads = attend(x, grid_qkv, value_t, bias, 1)
            heads_buf[pl.ds(start, 4)] = heads.reshape(4, CELLS, width)
            return carry

        lax.fori_loop(0, 2, groups, 0)
        for chunk in range(4):
            rows = jnp.concatenate(
                [
                    heads_buf[
                        :, chunk * 16 : (chunk + 1) * 16, half * half_width : (half + 1) * half_width
                    ].reshape(128, half_width)
                    for half in range(2)
                ],
                axis=0,
            )
            answers[b, chunk * 16 : (chunk + 1) * 16] = (
                dot_nn(perm[1], rows).astype(BF16).reshape(16, 16, half_width)
            )

        pltpu.make_async_copy(answers.at[b, me], returned.at[b, me], back_recv.at[b]).start()

        def post(i, carry):
            target = lax.rem(me + i, CELLS)
            pltpu.make_async_remote_copy(
                src_ref=answers.at[b, target],
                dst_ref=returned.at[b, me],
                send_sem=back_send.at[b],
                recv_sem=back_recv.at[b],
                device_id=device(target),
                device_id_type=MESH,
            ).start()
            return carry

        lax.fori_loop(1, CELLS, post, 0)
        return carry

    lax.fori_loop(0, batch, grid, 0)
    loads[5].wait()
    loads[6].wait()
    loads[7].wait()
    gain = gain_ref[...]

    def mlp(step, carry):
        b, half = step // 2, lax.rem(step, 2)

        @pl.when(half == 0)
        def _():
            pltpu.make_async_copy(returned.at[b], returned.at[b], back_recv.at[b]).wait()

        packed = returned[b, pl.ds(pl.multiple_of(half * 32, 32), 32)].astype(F32)
        heads = jnp.concatenate([packed[:, :8], packed[:, 8:]], axis=2)
        heads = heads.reshape(4 * CELLS, width).astype(BF16)
        start = half * 4
        total = res[b, pl.ds(start, 4)].reshape(4 * CELLS, width) + dot_nn(heads, grid_out[...])
        normed = (layer_norm(total) * gain).astype(BF16)
        cut = 512
        for i in range(mlp_in.shape[1] // cut):
            inner = dot_nn(normed, mlp_in[:, i * cut : (i + 1) * cut])
            cubic = inner + 0.044715 * (inner * inner * inner)
            hidden = 0.5 * inner * (1.0 + jnp.tanh(math.sqrt(2.0 / math.pi) * cubic))
            total = total + dot_nn(hidden.astype(BF16), mlp_out[i * cut : (i + 1) * cut, :])
        res[b, pl.ds(start, 4)] = total.reshape(4, WIN, WIN, width)
        pltpu.make_async_copy(
            res.at[b, pl.ds(start, 4)], out_ref.at[b, pl.ds(start, 4)], out_sem
        ).start()
        return carry

    lax.fori_loop(0, 2 * batch, mlp, 0)
    for copy in sends:
        copy.wait_send()
    for b in range(batch):
        part = received.at[b, pl.ds(0, CELLS - 1)]
        pltpu.make_async_copy(part, part, there_send.at[b]).wait()
        pltpu.make_async_copy(part, part, back_send.at[b]).wait()
    pltpu.make_async_copy(res, out_ref, out_sem).wait()


def on_device(
    latent,
    context,
    conv_weight,
    window_qkv,
    window_out,
    window_bias,
    grid_qkv,
    grid_out,
    grid_bias,
    mlp_gain,
    mlp_in,
    mlp_out,
):
    samples, row_count, col_count, channels = latent.shape
    tables = jnp.stack([window_bias, grid_bias]).transpose(0, 2, 3, 1)
    tables = jnp.pad(tables, ((0, 0), (0, 0), (0, 1), (0, 0))).reshape(2, 240, 16)
    tiles = latent.reshape(samples, row_count, col_count // WIN, WIN, channels)
    vmem = pltpu.VMEM
    dma = pltpu.SemaphoreType.DMA
    any_spec = pl.BlockSpec(memory_space=pl.ANY)
    vmem_spec = pl.BlockSpec(memory_space=pltpu.VMEM)
    slots = (samples, CELLS, 2 * WIN, channels // 2)
    result = pl.pallas_call(
        block_kernel,
        out_shape=jax.ShapeDtypeStruct(tiles.shape, F32),
        in_specs=[any_spec] * 9 + [vmem_spec] * 2,
        out_specs=any_spec,
        scratch_shapes=[
            vmem(tiles.shape, F32),
            vmem((samples, 8, 64, context.shape[3]), BF16),
            vmem(conv_weight.shape, BF16),
            vmem(window_qkv.shape, BF16),
            vmem(window_out.shape, BF16),
            vmem(grid_qkv.shape, BF16),
            vmem(grid_out.shape, BF16),
            vmem(mlp_in.shape, BF16),
            vmem(mlp_out.shape, BF16),
            vmem((2, channels, channels), BF16),
            vmem((row_count * col_count, 6 * CTX_COLS), BF16),
            vmem((2, 4, CELLS, 256), F32),
            vmem((240, 1024), F32),
            vmem((15, 8, 1024), F32),
            vmem((2, 256, 256), BF16),
            vmem((samples, WIN, WIN, 2 * WIN, channels // 2), BF16),
            vmem(slots, BF16),
            vmem(slots, BF16),
            vmem(slots, BF16),
            vmem((WIN, CELLS, channels), BF16),
            vmem((WIN, CELLS, channels), BF16),
            dma((8,)),
            dma((8,)),
            dma,
            dma((samples,)),
            dma((samples,)),
            dma((samples,)),
            dma((samples,)),
            dma,
        ],
        compiler_params=pltpu.CompilerParams(
            collective_id=0, has_side_effects=True, vmem_limit_bytes=56 * 2**20
        ),
        cost_estimate=pl.CostEstimate(
            flops=10_000_000_000, bytes_accessed=16_000_000, transcendentals=4_000_000
        ),
    )(
        tiles,
        context,
        conv_weight,
        window_qkv,
        window_out,
        grid_qkv,
        grid_out,
        mlp_in,
        mlp_out,
        tables,
        mlp_gain.reshape(1, channels),
    )
    return result.reshape(latent.shape)


def solution(mesh):
    return jax.shard_map(
        on_device,
        mesh=mesh,
        in_specs=(
            P(None, "wide", "narrow", None),
            P(None, "wide", "narrow", None),
            P(),
            P(),
            P(),
            P(),
            P(),
            P(),
            P(),
            P(),
            P(),
            P(),
        ),
        out_specs=P(None, "wide", "narrow", None),
        check_vma=False,
    )
```

profile of v0, /device:TPU:5, one launch (start us, length us, event | category | flops | bytes accessed | tf_op | source)
XLA Modules:
  0.0 89.5 jit_solution(9013767991365016989)
XLA Ops:
  0.0 1.0 %maximum_bitcast_fusion = f32[2,15,15,16]{2,3,1,0:T(8,128)S(1)} fusion(f32[1,16,15,15]{3,1,2,0:T(8,128)} %bitcast.10, f32[1,16,15,15]{3,1,2,0:T(8,128)} %bitcast.11), kind=kLoop, calls=%fused_computation | loop fusion | flops 7200 | bytes 57600 | tf_op jit(solution)/shard_map/transpose | solution.py:471
  1.0 0.2 copy.14
  1.2 0.7 pad.4.clone
  2.0 84.4 %shard_map.118 = f32[2,8,8,8,512]{4,3,2,1,0:T(8,128)} custom-call(f32[2,8,8,8,512]{4,3,2,1,0:T(8,128)} %bitcast.12, bf16[2,4,32,256]{3,2,1,0:T(8,128)(2,1)} %context_ref.1, bf16[3,3,256,512]{3,2,1,0:T(8,128)(2,1)} %conv_hbm.1, bf16[512,1536]{1,0:T(8,128)(2,1)} %window_qkv_hbm.1, bf16[512,512]{1,0:T(8,128)(2,1)} %window_out_hbm.1, ...), custom_call_target="tpu_custom_call" | custom-call | flops 10000000000 | bytes 16000000 | tf_op jit(solution)/shard_map/pallas_call | solution.py:479
  86.4 3.1 %copy.16 = f32[2,8,64,512]{3,2,1,0:T(8,128)} copy(f32[2,8,64,512]{3,2,1,0:T(8,128)} %bitcast.8) | data formatting | bytes 4194304
where the time goes:
time: 89.9 us; the launch traced here: 89.5 us
  Pallas kernels  84.4 us (94%)
  local copies, waits for them, and re-layouts  4.12 us (5%)
  other arithmetic  0.98 us (1%)
    pallas_call x1, Pallas kernels, on_device(): pl.pallas_call(block_kernel, out_shape=jax.ShapeDtypeStruct(tiles.shape,...  84.4 us
    unnamed x2, local copies, waits for them, and re-layouts  3.39 us

commit v1 on v0

--- a/solution.py
+++ b/solution.py
@@ -16,6 +16,7 @@
 CELLS = WIN * WIN
 LOG2E = 1.4426950408889634
 CTX_COLS = 48
+GROUP_BATCH = 4
 
 
 def iota(shape, dim):
@@ -64,11 +65,24 @@
         up_ref[pl.ds(start, block), :] = (row_weight * col_weight).astype(BF16)
 
 
+def three_terms(values):
+    high = values.astype(BF16)
+    rest = values - high.astype(F32)
+    middle = rest.astype(BF16)
+    return high, middle, (rest - middle.astype(F32)).astype(BF16)
+
+
 def fill_bias(table, which, spread_ref, step_ref, bias_ref):
-    pick = jnp.where(iota((16, 1024), 0) == (iota((16, 1024), 1) >> 6), 1.0, 0.0)
-    spread_ref[...] = (
-        jnp.dot(table, pick, preferred_element_type=F32, precision=lax.Precision.HIGHEST) * LOG2E
-    )
+    turn = jnp.where(iota((16, 15), 0) == iota((16, 15), 1), 1.0, 0.0).astype(BF16)
+    pick = jnp.where((iota((240, 1024), 0) & 15) == (iota((240, 1024), 1) >> 6), 1.0, 0.0)
+    pick = pick.astype(BF16)
+    step_of_lane = iota((16, 240), 1) >> 4
+    total = jnp.zeros((240, 1024), F32)
+    for term in three_terms(table.reshape(240, 15)):
+        turned = dot_nt(turn, term)
+        apart = [jnp.where(step_of_lane == a, turned, 0.0).astype(BF16) for a in range(15)]
+        total = total + dot_nn(jnp.concatenate(apart, axis=0), pick)
+    spread_ref[...] = total * LOG2E
     col_step = (iota((8, 1024), 1) & 7) - iota((8, 1024), 0) + 7
 
     def one_row_step(a, carry):
@@ -97,20 +111,21 @@
 
 def attend(x, qkv_ref, value_ref, bias_ref, which):
     width = x.shape[1]
+    count = x.shape[0] // CELLS
     queries = dot_nn(x, qkv_ref[:, 0:width]).astype(BF16)
     keys = dot_nn(x, qkv_ref[:, width : 2 * width]).astype(BF16)
     values = dot_nt(value_ref[which], x).astype(BF16)
     head_of_lane = iota((CELLS, 128), 1) >> 5
     head_masks = [jnp.where(head_of_lane == h, 1.0, 0.0).astype(BF16) for h in range(4)]
-    group_of_lane = iota((128, 256), 1) >> 6
-    group_masks = [jnp.where(group_of_lane == g, 1.0, 0.0).astype(BF16) for g in range(4)]
+    group_of_lane = iota((128, count * CELLS), 1) >> 6
+    group_masks = [jnp.where(group_of_lane == g, 1.0, 0.0).astype(BF16) for g in range(count)]
     low = iota((HEAD, 128), 1) < 64
     outs = []
     for block in range(width // 128):
         lanes = slice(block * 128, (block + 1) * 128)
         bias = bias_ref[which, block]
         weights = []
-        for g in range(4):
+        for g in range(count):
             rows = slice(g * CELLS, (g + 1) * CELLS)
             query = queries[rows, lanes]
             spread = jnp.concatenate([query * mask for mask in head_masks], axis=0)
@@ -124,7 +139,7 @@
         blended = dot_nn(stacked, weight)
         for h in range(4):
             picked = []
-            for pair in range(2):
+            for pair in range(count // 2):
                 parts = []
                 for g in (2 * pair, 2 * pair + 1):
                     parts.append(
@@ -140,7 +155,7 @@
                     picked.append(jnp.where(low, pltpu.roll(first, 64, 1), second))
             outs.append(jnp.concatenate(picked, axis=1).astype(BF16))
     turned = jnp.concatenate(outs, axis=0)
-    return dot_nt(identity(4 * CELLS), turned).astype(BF16)
+    return dot_nt(identity(count * CELLS), turned).astype(BF16)
 
 
 def block_kernel(
@@ -153,11 +168,14 @@
     grid_out_hbm,
     mlp_in_hbm,
     mlp_out_hbm,
-    table_ref,
+    window_table,
+    grid_table,
     gain_ref,
     out_ref,
     res,
     halo,
+    edge_out,
+    edge_in,
     conv_w,
     window_qkv,
     window_out,
@@ -178,8 +196,11 @@
     grouped,
     heads_buf,
     load_sem,
-    halo_send,
-    halo_recv,
+    own_sem,
+    row_send,
+    row_recv,
+    edge_send,
+    edge_recv,
     there_send,
     there_recv,
     back_send,
@@ -213,8 +234,14 @@
             )
         )
     ]
-    own = pltpu.make_async_copy(context_ref, halo.at[:, pl.ds(2, 4), pl.ds(16, 32), :], halo_recv)
+    half_rows, half_cols = context_ref.shape[1], context_ref.shape[2]
+    depth = context_ref.shape[3]
+    batch = latent_ref.shape[0]
+    own = pltpu.make_async_copy(context_ref, halo.at[:, pl.ds(2, half_rows)], own_sem)
     own.start()
+    edge_in[...] = jnp.zeros_like(edge_in)
+    for load in loads:
+        load.start()
 
     barrier = pltpu.get_barrier_semaphore()
 
@@ -223,12 +250,6 @@
             barrier, inc=1, device_id=device(lax.rem(me + i, CELLS)), device_id_type=MESH
         )
         return carry
-
-    around = []
-    for dw in (-1, 0, 1):
-        for dn in (-1, 0, 1):
-            if dw or dn:
-                around.append((dw, dn))
 
     def neighbour(dw, dn):
         return (
@@ -236,57 +257,92 @@
             lax.rem(narrow + dn + narrow_count, narrow_count),
         )
 
-    for dw, dn in around:
-        if dw:
+    for dw in (-1, 1):
+        for dn in (0, -1, 1):
             pl.semaphore_signal(barrier, inc=1, device_id=neighbour(dw, dn), device_id_type=MESH)
     lax.fori_loop(1, CELLS, greet, 0)
-    for load in loads:
-        load.start()
+
+    own.wait()
+    for side in range(2):
+        strip = halo[:, 2 : 2 + half_rows, side * 16 : side * 16 + 16, :].reshape(
+            batch * half_rows * 16, depth
+        )
+        row = iota((16, batch * half_rows * 16), 0)
+        pick = iota((16, batch * half_rows * 16), 1) == (row >> 1) * 16 + (row & 1) + 14 * side
+        edge_out[side] = dot_nn(jnp.where(pick, 1.0, 0.0).astype(BF16), strip).astype(BF16)
     pl.semaphore_wait(barrier, CELLS - 1 + 6)
 
-    sends = []
-    row_cut = {-1: (0, 2, 6), 0: (0, 4, 2), 1: (2, 2, 0)}
-    col_cut = {-1: (0, 16, 48), 0: (0, 32, 16), 1: (16, 16, 0)}
-    for dw, dn in around:
-        row_from, rows, row_to = row_cut[dw]
-        col_from, cols, col_to = col_cut[dn]
-        copy = pltpu.make_async_remote_copy(
-            src_ref=context_ref.at[:, pl.ds(row_from, rows), pl.ds(col_from, cols), :],
-            dst_ref=halo.at[:, pl.ds(row_to, rows), pl.ds(col_to, cols), :],
-            send_sem=halo_send.at[len(sends)],
-            recv_sem=halo_recv,
+    def exists(dw, dn):
+        return (
+            (wide + dw >= 0)
+            & (wide + dw < wide_count)
+            & (narrow + dn >= 0)
+            & (narrow + dn < narrow_count)
+        )
+
+    def row_copy(b, dw):
+        lane = (dw + 1) // 2
+        return pltpu.make_async_remote_copy(
+            src_ref=context_ref.at[b, pl.ds(half_rows - 2 if dw > 0 else 0, 2)],
+            dst_ref=halo.at[b, pl.ds(0 if dw > 0 else half_rows + 2, 2)],
+            send_sem=row_send.at[b, lane],
+            recv_sem=row_recv.at[b, lane],
+            device_id=neighbour(dw, 0),
+            device_id_type=MESH,
+        )
+
+    def edge_copy(dw, dn):
+        side = (dn + 1) // 2
+        return pltpu.make_async_remote_copy(
+            src_ref=edge_out.at[side],
+            dst_ref=edge_in.at[1 - side, 1 - dw],
+            send_sem=edge_send.at[side, 1 - dw],
+            recv_sem=edge_recv.at[1 - side, 1 - dw],
             device_id=neighbour(dw, dn),
             device_id_type=MESH,
         )
-        copy.start()
-        sends.append(copy)
-
+
+    edges = [(dw, dn) for dn in (-1, 1) for dw in (-1, 0, 1)]
+    for dw in (-1, 1):
+        pl.when(exists(dw, 0))(row_copy(0, dw).start)
+    for dw, dn in edges:
+        pl.when(exists(dw, dn))(edge_copy(dw, dn).start)
+    for b in range(1, batch):
+        for dw in (-1, 1):
+            pl.when(exists(dw, 0))(row_copy(b, dw).start)
+
+    fill_bias(window_table[...], 0, spread, steps, bias)
     fill_upsampler(up)
-    out_row = iota((256, 256), 0)
-    in_row = iota((256, 256), 1)
-    perm[0] = jnp.where(
-        in_row == (out_row & 15) * 16 + (out_row >> 7) * 8 + ((out_row >> 4) & 7), 1.0, 0.0
-    ).astype(BF16)
-    perm[1] = jnp.where(
-        out_row == (in_row & 15) * 16 + (in_row >> 7) * 8 + ((in_row >> 4) & 7), 1.0, 0.0
-    ).astype(BF16)
-    fill_bias(table_ref[0], 0, spread, steps, bias)
-    fill_bias(table_ref[1], 1, spread, steps, bias)
     width = window_out.shape[0]
     loads[2].wait()
     value_t[0] = dot_nt(identity(width), window_qkv[:, 2 * width :]).astype(BF16)
-    loads[4].wait()
-    value_t[1] = dot_nt(identity(width), grid_qkv[:, 2 * width :]).astype(BF16)
-
-    pltpu.make_async_copy(halo, halo, halo_recv).wait()
+    for dw, dn in edges:
+        pl.when(exists(-dw, -dn))(edge_copy(dw, dn).wait_recv)
     loads[0].wait()
     loads[1].wait()
-    depth = context_ref.shape[3]
-    half_rows, half_cols = context_ref.shape[1], context_ref.shape[2]
-    batch = latent_ref.shape[0]
-
-    def convolve(b, carry):
-        widened = halo[b].astype(F32)[:, 8:56, :]
+    loads[3].wait()
+    def convolve(b):
+        for dw in (-1, 1):
+            lane = (dw + 1) // 2
+            arrived = halo.at[b, pl.ds(0 if dw > 0 else half_rows + 2, 2)]
+            pl.when(exists(-dw, 0))(
+                pltpu.make_async_copy(arrived, arrived, row_recv.at[b, lane]).wait
+            )
+        sides = []
+        place, taken = iota((64, 48), 0), iota((64, 48), 1)
+        row, col = place >> 3, place & 7
+        slot = jnp.where(row < 2, 0, jnp.where(row < 2 + half_rows, 1, 2))
+        their_row = jnp.where(row < 2, row + half_rows - 2, row - 2)
+        their_row = jnp.where(row < 2 + half_rows, their_row, row - 2 - half_rows)
+        base = slot * 16 + b * (2 * half_rows) + their_row * 2
+        for side in range(2):
+            first = 6 if side == 0 else 0
+            chosen = (taken == base + col - first) & (col >= first) & (col < first + 2)
+            strip = dot_nn(
+                jnp.where(chosen, 1.0, 0.0).astype(BF16), edge_in[side].reshape(48, depth)
+            )
+            sides.append(strip.reshape(8, 8, depth))
+        widened = jnp.concatenate([sides[0], halo[b].astype(F32), sides[1]], axis=1)
         shape = (8, CTX_COLS, depth)
         row_place = wide * half_rows - 2 + iota(shape, 0)
         col_place = narrow * half_cols - 8 + iota(shape, 1)
@@ -314,53 +370,67 @@
         )
         features = jnp.where(inside.reshape(rows, width), total, 0.0).astype(BF16)
         res[b] = res[b] + dot_nn(up[...], features).reshape(res.shape[1:])
-        return carry
-
-    lax.fori_loop(0, batch, convolve, 0)
-    loads[3].wait()
-
-    def windows(step, carry):
-        b, half = step // 2, lax.rem(step, 2)
-        places = [lax.rem(narrow + half * 4 + i, WIN) for i in range(4)]
+
+    def windows(b, part):
+        per_part = GROUP_BATCH
+        places = []
+        for i in range(per_part):
+            turn = part * per_part + i
+            places.append(lax.rem(narrow + lax.rem(turn, 4) * 2 + turn // 4, WIN))
         before = jnp.concatenate([res[b, :, place].reshape(CELLS, width) for place in places], axis=0)
         normed = layer_norm(before).astype(BF16)
         heads = attend(normed, window_qkv, value_t, bias, 0)
         after = before + dot_nn(heads, window_out[...])
-        normed = layer_norm(after).reshape(4, WIN, WIN, width)
+        normed = layer_norm(after).reshape(per_part, WIN, WIN, width)
         for i, place in enumerate(places):
-            res[b, :, place] = after[i * CELLS : (i + 1) * CELLS].reshape(WIN, WIN, width)
             sent[b, place] = jnp.concatenate(
                 [normed[i, :, :, : width // 2], normed[i, :, :, width // 2 :]], axis=1
             ).astype(BF16)
-
-        def post(i, carry):
-            place = lax.rem(narrow + half * 4 + i // WIN, WIN)
-            row = lax.rem(my_row + lax.rem(i, WIN), WIN)
-            target = row * WIN + place
-
-            @pl.when(target == me)
-            def _():
-                pltpu.make_async_copy(
-                    sent.at[b, place, row], received.at[b, me], there_recv.at[b]
-                ).start()
-
-            @pl.when(target != me)
-            def _():
-                pltpu.make_async_remote_copy(
+            for j in range(WIN):
+                row = lax.rem(my_row + j, WIN)
+                target = row * WIN + place
+                away = pltpu.make_async_remote_copy(
                     src_ref=sent.at[b, place, row],
                     dst_ref=received.at[b, me],
                     send_sem=there_send.at[b],
                     recv_sem=there_recv.at[b],
                     device_id=device(target),
                     device_id_type=MESH,
-                ).start()
-
+                )
+                if i or j:
+                    away.start()
+                else:
+                    stays = pltpu.make_async_copy(
+                        sent.at[b, place, row], received.at[b, me], there_recv.at[b]
+                    )
+                    pl.when(target == me)(stays.start)
+                    pl.when(target != me)(away.start)
+        for i, place in enumerate(places):
+            res[b, :, place] = after[i * CELLS : (i + 1) * CELLS].reshape(WIN, WIN, width)
+
+    def sample(b, carry):
+        convolve(b)
+
+        def part(half, carry):
+            windows(b, half)
             return carry
 
-        lax.fori_loop(0, 4 * WIN, post, 0)
+        lax.fori_loop(0, WIN // GROUP_BATCH, part, 0)
         return carry
 
-    lax.fori_loop(0, 2 * batch, windows, 0)
+    lax.fori_loop(0, batch, sample, 0)
+
+    out_row = iota((256, 256), 0)
+    in_row = iota((256, 256), 1)
+    perm[0] = jnp.where(
+        in_row == (out_row & 15) * 16 + (out_row >> 7) * 8 + ((out_row >> 4) & 7), 1.0, 0.0
+    ).astype(BF16)
+    perm[1] = jnp.where(
+        out_row == (in_row & 15) * 16 + (in_row >> 7) * 8 + ((in_row >> 4) & 7), 1.0, 0.0
+    ).astype(BF16)
+    fill_bias(grid_table[...], 1, spread, steps, bias)
+    loads[4].wait()
+    value_t[1] = dot_nt(identity(width), grid_qkv[:, 2 * width :]).astype(BF16)
 
     def grid(b, carry):
         pltpu.make_async_copy(received.at[b], received.at[b], there_recv.at[b]).wait()
@@ -381,35 +451,34 @@
             return carry
 
         lax.fori_loop(0, 2, groups, 0)
-        for chunk in range(4):
+        for turn in range(4):
+            chunk = lax.rem(me // 16 + turn, 4)
+            cut = pl.ds(pl.multiple_of(chunk * 16, 16), 16)
             rows = jnp.concatenate(
                 [
-                    heads_buf[
-                        :, chunk * 16 : (chunk + 1) * 16, half * half_width : (half + 1) * half_width
-                    ].reshape(128, half_width)
+                    heads_buf[:, cut, half * half_width : (half + 1) * half_width].reshape(
+                        128, half_width
+                    )
                     for half in range(2)
                 ],
                 axis=0,
             )
-            answers[b, chunk * 16 : (chunk + 1) * 16] = (
-                dot_nn(perm[1], rows).astype(BF16).reshape(16, 16, half_width)
-            )
-
-        pltpu.make_async_copy(answers.at[b, me], returned.at[b, me], back_recv.at[b]).start()
-
-        def post(i, carry):
-            target = lax.rem(me + i, CELLS)
-            pltpu.make_async_remote_copy(
-                src_ref=answers.at[b, target],
-                dst_ref=returned.at[b, me],
-                send_sem=back_send.at[b],
-                recv_sem=back_recv.at[b],
-                device_id=device(target),
-                device_id_type=MESH,
-            ).start()
-            return carry
-
-        lax.fori_loop(1, CELLS, post, 0)
+            answers[b, cut] = dot_nn(perm[1], rows).astype(BF16).reshape(16, 16, half_width)
+            for i in range(16):
+                target = chunk * 16 + lax.rem(me + i, 16)
+                if turn or i:
+                    pltpu.make_async_remote_copy(
+                        src_ref=answers.at[b, target],
+                        dst_ref=returned.at[b, me],
+                        send_sem=back_send.at[b],
+                        recv_sem=back_recv.at[b],
+                        device_id=device(target),
+                        device_id_type=MESH,
+                    ).start()
+                else:
+                    pltpu.make_async_copy(
+                        answers.at[b, me], returned.at[b, me], back_recv.at[b]
+                    ).start()
         return carry
 
     lax.fori_loop(0, batch, grid, 0)
@@ -444,8 +513,11 @@
         return carry
 
     lax.fori_loop(0, 2 * batch, mlp, 0)
-    for copy in sends:
-        copy.wait_send()
+    for dw, dn in edges:
+        pl.when(exists(dw, dn))(edge_copy(dw, dn).wait_send)
+    for b in range(batch):
+        for dw in (-1, 1):
+            pl.when(exists(dw, 0))(row_copy(b, dw).wait_send)
     for b in range(batch):
         part = received.at[b, pl.ds(0, CELLS - 1)]
         pltpu.make_async_copy(part, part, there_send.at[b]).wait()
@@ -468,8 +540,6 @@
     mlp_out,
 ):
     samples, row_count, col_count, channels = latent.shape
-    tables = jnp.stack([window_bias, grid_bias]).transpose(0, 2, 3, 1)
-    tables = jnp.pad(tables, ((0, 0), (0, 0), (0, 1), (0, 0))).reshape(2, 240, 16)
     tiles = latent.reshape(samples, row_count, col_count // WIN, WIN, channels)
     vmem = pltpu.VMEM
     dma = pltpu.SemaphoreType.DMA
@@ -479,11 +549,13 @@
     result = pl.pallas_call(
         block_kernel,
         out_shape=jax.ShapeDtypeStruct(tiles.shape, F32),
-        in_specs=[any_spec] * 9 + [vmem_spec] * 2,
+        in_specs=[any_spec] * 9 + [vmem_spec] * 3,
         out_specs=any_spec,
         scratch_shapes=[
             vmem(tiles.shape, F32),
-            vmem((samples, 8, 64, context.shape[3]), BF16),
+            vmem((samples, 8, 32, context.shape[3]), BF16),
+            vmem((2, 16, context.shape[3]), BF16),
+            vmem((2, 3, 16, context.shape[3]), BF16),
             vmem(conv_weight.shape, BF16),
             vmem(window_qkv.shape, BF16),
             vmem(window_out.shape, BF16),
@@ -504,8 +576,11 @@
             vmem((WIN, CELLS, channels), BF16),
             vmem((WIN, CELLS, channels), BF16),
             dma((8,)),
-            dma((8,)),
             dma,
+            dma((samples, 2)),
+            dma((samples, 2)),
+            dma((2, 3)),
+            dma((2, 3)),
             dma((samples,)),
             dma((samples,)),
             dma((samples,)),
@@ -528,7 +603,8 @@
         grid_out,
         mlp_in,
         mlp_out,
-        tables,
+        window_bias.transpose(1, 0, 2),
+        grid_bias.transpose(1, 0, 2),
         mlp_gain.reshape(1, channels),
     )
     return result.reshape(latent.shape)

time: 89.9 us -> 82.2 us (0.914)
  Pallas kernels: 84.4 us -> 78.9 us
  other arithmetic: 0.98 us -> 0 us
  local copies, waits for them, and re-layouts: 4.12 us -> 3.14 us
    pallas_call x1, Pallas kernels: 84.4 us -> 78.9 us  [on_device(): pl.pallas_call(block_kernel, out_shape=jax.ShapeDtypeStruct(tiles.shape,...]
    transpose x1 -> x0, other arithmetic: 0.98 us -> none  [on_device(): tables = jnp.stack([window_bias, grid_bias]).transpose(0, 2, 3, 1)]
    unnamed x2 -> x1, local copies, waits for them, and re-layouts: 3.39 us -> 3.14 us
where the time goes in v1:
time: 82.2 us; the launch traced here: 82.1 us
  Pallas kernels  78.9 us (96%)
  local copies, waits for them, and re-layouts  3.14 us (4%)
    pallas_call x1, Pallas kernels, on_device(): pl.pallas_call(block_kernel, out_shape=jax.ShapeDtypeStruct(tiles.shape,...  78.9 us
    unnamed x1, local copies, waits for them, and re-layouts  3.14 us

profile of v1, /device:TPU:5, one launch (start us, length us, event | category | flops | bytes accessed | tf_op | source)
XLA Modules:
  0.0 82.1 jit_solution(11304354798491325831)
XLA Ops:
  0.0 78.9 %shard_map.118 = f32[2,8,8,8,512]{4,3,2,1,0:T(8,128)} custom-call(f32[2,8,8,8,512]{4,3,2,1,0:T(8,128)} %bitcast.6, bf16[2,4,32,256]{3,2,1,0:T(8,128)(2,1)} %context_ref.1, bf16[3,3,256,512]{3,2,1,0:T(8,128)(2,1)} %conv_hbm.1, bf16[512,1536]{1,0:T(8,128)(2,1)} %window_qkv_hbm.1, bf16[512,512]{1,0:T(8,128)(2,1)} %window_out_hbm.1, ...), custom_call_target="tpu_custom_call" | custom-call | flops 10000000000 | bytes 16000000 | tf_op jit(solution)/shard_map/pallas_call | solution.py:549
  78.9 3.1 %copy.14 = f32[2,8,64,512]{3,2,1,0:T(8,128)} copy(f32[2,8,64,512]{3,2,1,0:T(8,128)} %bitcast.5) | data formatting | bytes 4194304

commit v2 on v1

--- a/solution.py
+++ b/solution.py
@@ -240,8 +240,6 @@
     own = pltpu.make_async_copy(context_ref, halo.at[:, pl.ds(2, half_rows)], own_sem)
     own.start()
     edge_in[...] = jnp.zeros_like(edge_in)
-    for load in loads:
-        load.start()
 
     barrier = pltpu.get_barrier_semaphore()
 
@@ -260,16 +258,12 @@
     for dw in (-1, 1):
         for dn in (0, -1, 1):
             pl.semaphore_signal(barrier, inc=1, device_id=neighbour(dw, dn), device_id_type=MESH)
-    lax.fori_loop(1, CELLS, greet, 0)
+    for i in (CELLS - 1, *range(1, CELLS - 1)):
+        greet(i, 0)
+    for load in loads[:4]:
+        load.start()
 
     own.wait()
-    for side in range(2):
-        strip = halo[:, 2 : 2 + half_rows, side * 16 : side * 16 + 16, :].reshape(
-            batch * half_rows * 16, depth
-        )
-        row = iota((16, batch * half_rows * 16), 0)
-        pick = iota((16, batch * half_rows * 16), 1) == (row >> 1) * 16 + (row & 1) + 14 * side
-        edge_out[side] = dot_nn(jnp.where(pick, 1.0, 0.0).astype(BF16), strip).astype(BF16)
     pl.semaphore_wait(barrier, CELLS - 1 + 6)
 
     def exists(dw, dn):
@@ -283,7 +277,7 @@
     def row_copy(b, dw):
         lane = (dw + 1) // 2
         return pltpu.make_async_remote_copy(
-            src_ref=context_ref.at[b, pl.ds(half_rows - 2 if dw > 0 else 0, 2)],
+            src_ref=halo.at[b, pl.ds(half_rows if dw > 0 else 2, 2)],
             dst_ref=halo.at[b, pl.ds(0 if dw > 0 else half_rows + 2, 2)],
             send_sem=row_send.at[b, lane],
             recv_sem=row_recv.at[b, lane],
@@ -305,11 +299,21 @@
     edges = [(dw, dn) for dn in (-1, 1) for dw in (-1, 0, 1)]
     for dw in (-1, 1):
         pl.when(exists(dw, 0))(row_copy(0, dw).start)
+    for side in range(2):
+        strip = halo[:, 2 : 2 + half_rows, side * 16 : side * 16 + 16, :].reshape(
+            batch * half_rows * 16, depth
+        )
+        row = iota((16, batch * half_rows * 16), 0)
+        pick = iota((16, batch * half_rows * 16), 1) == (row >> 1) * 16 + (row & 1) + 14 * side
+        edge_out[side] = dot_nn(jnp.where(pick, 1.0, 0.0).astype(BF16), strip).astype(BF16)
     for dw, dn in edges:
         pl.when(exists(dw, dn))(edge_copy(dw, dn).start)
     for b in range(1, batch):
         for dw in (-1, 1):
             pl.when(exists(dw, 0))(row_copy(b, dw).start)
+
+    for load in loads[4:]:
+        load.start()
 
     fill_bias(window_table[...], 0, spread, steps, bias)
     fill_upsampler(up)
@@ -488,31 +492,27 @@
     gain = gain_ref[...]
 
     def mlp(step, carry):
-        b, half = step // 2, lax.rem(step, 2)
-
-        @pl.when(half == 0)
-        def _():
-            pltpu.make_async_copy(returned.at[b], returned.at[b], back_recv.at[b]).wait()
-
-        packed = returned[b, pl.ds(pl.multiple_of(half * 32, 32), 32)].astype(F32)
+        b = step
+        pltpu.make_async_copy(returned.at[b], returned.at[b], back_recv.at[b]).wait()
+        packed = returned[b].astype(F32)
         heads = jnp.concatenate([packed[:, :8], packed[:, 8:]], axis=2)
-        heads = heads.reshape(4 * CELLS, width).astype(BF16)
-        start = half * 4
-        total = res[b, pl.ds(start, 4)].reshape(4 * CELLS, width) + dot_nn(heads, grid_out[...])
+        heads = heads.reshape(8 * CELLS, width).astype(BF16)
+        start = 0
+        total = res[b].reshape(8 * CELLS, width) + dot_nn(heads, grid_out[...])
         normed = (layer_norm(total) * gain).astype(BF16)
-        cut = 512
+        cut = 256
         for i in range(mlp_in.shape[1] // cut):
             inner = dot_nn(normed, mlp_in[:, i * cut : (i + 1) * cut])
             cubic = inner + 0.044715 * (inner * inner * inner)
             hidden = 0.5 * inner * (1.0 + jnp.tanh(math.sqrt(2.0 / math.pi) * cubic))
             total = total + dot_nn(hidden.astype(BF16), mlp_out[i * cut : (i + 1) * cut, :])
-        res[b, pl.ds(start, 4)] = total.reshape(4, WIN, WIN, width)
+        res[b] = total.reshape(8, WIN, WIN, width)
         pltpu.make_async_copy(
-            res.at[b, pl.ds(start, 4)], out_ref.at[b, pl.ds(start, 4)], out_sem
+            res.at[b], out_ref.at[b], out_sem
         ).start()
         return carry
 
-    lax.fori_loop(0, 2 * batch, mlp, 0)
+    lax.fori_loop(0, batch, mlp, 0)
     for dw, dn in edges:
         pl.when(exists(dw, dn))(edge_copy(dw, dn).wait_send)
     for b in range(batch):
@@ -523,6 +523,26 @@
         pltpu.make_async_copy(part, part, there_send.at[b]).wait()
         pltpu.make_async_copy(part, part, back_send.at[b]).wait()
     pltpu.make_async_copy(res, out_ref, out_sem).wait()
+
+
+def copy_kernel(source_ref, target_ref, held, in_sem, out_sem):
+    batch, rows = held.shape[0], held.shape[1]
+    pieces = [(b, pl.ds(row, 2)) for b in range(batch) for row in range(0, rows, 2)]
+    loads = [
+        pltpu.make_async_copy(source_ref.at[piece], held.at[piece], in_sem.at[i])
+        for i, piece in enumerate(pieces)
+    ]
+    stores = [
+        pltpu.make_async_copy(held.at[piece], target_ref.at[piece], out_sem.at[i])
+        for i, piece in enumerate(pieces)
+    ]
+    for load in loads:
+        load.start()
+    for load, store in zip(loads, stores):
+        load.wait()
+        store.start()
+    for store in stores:
+        store.wait()
 
 
 def on_device(
@@ -607,6 +627,14 @@
         grid_bias.transpose(1, 0, 2),
         mlp_gain.reshape(1, channels),
     )
+    result = pl.pallas_call(
+        copy_kernel,
+        out_shape=jax.ShapeDtypeStruct(tiles.shape, F32),
+        in_specs=[any_spec],
+        out_specs=any_spec,
+        scratch_shapes=[vmem(tiles.shape, F32), dma((4 * samples,)), dma((4 * samples,))],
+        compiler_params=pltpu.CompilerParams(vmem_limit_bytes=56 * 2**20),
+    )(result)
     return result.reshape(latent.shape)
 
 

time: 82.2 us -> 79.8 us (0.971)
  local copies, waits for them, and re-layouts: 3.14 us -> 0 us
    unnamed x1 -> x0, local copies, waits for them, and re-layouts: 3.14 us -> none
    pallas_call x0 -> x1, Pallas kernels: none -> 2.39 us  [on_device(): pl.pallas_call(copy_kernel, out_shape=jax.ShapeDtypeStruct(tiles.shape, F...]
    pallas_call x1, Pallas kernels: 78.9 us -> 77.3 us  [on_device(): pl.pallas_call(block_kernel, out_shape=jax.ShapeDtypeStruct(tiles.shape,...]
where the time goes in v2:
time: 79.8 us; the launch traced here: 79.7 us
  Pallas kernels  79.7 us (100%)
    pallas_call x1, Pallas kernels, on_device(): pl.pallas_call(block_kernel, out_shape=jax.ShapeDtypeStruct(tiles.shape,...  77.3 us
    pallas_call x1, Pallas kernels, on_device(): pl.pallas_call(copy_kernel, out_shape=jax.ShapeDtypeStruct(tiles.shape, F...  2.39 us

profile of v2, /device:TPU:5, one launch (start us, length us, event | category | flops | bytes accessed | tf_op | source)
XLA Modules:
  0.0 79.7 jit_solution(9830219451939965488)
XLA Ops:
  0.0 77.3 %shard_map.118.source_ref = f32[2,8,8,8,512]{4,3,2,1,0:T(8,128)} custom-call(f32[2,8,8,8,512]{4,3,2,1,0:T(8,128)} %bitcast.5, bf16[2,4,32,256]{3,2,1,0:T(8,128)(2,1)} %context_ref.1, bf16[3,3,256,512]{3,2,1,0:T(8,128)(2,1)} %conv_hbm.1, bf16[512,1536]{1,0:T(8,128)(2,1)} %window_qkv_hbm.1, bf16[512,512]{1,0:T(8,128)(2,1)} %window_out_hbm.1, ...), custom_call_target="tpu_custom_call" | custom-call | flops 10000000000 | bytes 16000000 | tf_op jit(solution)/shard_map/pallas_call | solution.py:569
  77.3 2.4 %shard_map.119 = f32[2,8,8,8,512]{4,3,2,1,0:T(8,128)} custom-call(f32[2,8,8,8,512]{4,3,2,1,0:T(8,128)} %shard_map.118.source_ref), custom_call_target="tpu_custom_call" | custom-call | tf_op jit(solution)/shard_map/pallas_call | solution.py:630

commit v3 on v2

--- a/solution.py
+++ b/solution.py
@@ -206,6 +206,7 @@
     back_send,
     back_recv,
     out_sem,
+    plane_sem,
 ):
     wide = lax.axis_index("wide")
     narrow = lax.axis_index("narrow")
@@ -243,11 +244,8 @@
 
     barrier = pltpu.get_barrier_semaphore()
 
-    def greet(i, carry):
-        pl.semaphore_signal(
-            barrier, inc=1, device_id=device(lax.rem(me + i, CELLS)), device_id_type=MESH
-        )
-        return carry
+    row_peers = [my_row * WIN + lax.rem(narrow + i, WIN) for i in (1, WIN - 1, *range(2, WIN - 1))]
+    column_peers = [lax.rem(my_row + i, WIN) * WIN + narrow for i in range(1, WIN)]
 
     def neighbour(dw, dn):
         return (
@@ -258,13 +256,13 @@
     for dw in (-1, 1):
         for dn in (0, -1, 1):
             pl.semaphore_signal(barrier, inc=1, device_id=neighbour(dw, dn), device_id_type=MESH)
-    for i in (CELLS - 1, *range(1, CELLS - 1)):
-        greet(i, 0)
+    for place in row_peers + column_peers:
+        pl.semaphore_signal(barrier, inc=1, device_id=device(place), device_id_type=MESH)
     for load in loads[:4]:
         load.start()
 
     own.wait()
-    pl.semaphore_wait(barrier, CELLS - 1 + 6)
+    pl.semaphore_wait(barrier, 2 * (WIN - 1) + 6)
 
     def exists(dw, dn):
         return (
@@ -312,6 +310,8 @@
         for dw in (-1, 1):
             pl.when(exists(dw, 0))(row_copy(b, dw).start)
 
+    for place in column_peers:
+        pl.semaphore_signal(plane_sem, inc=1, device_id=device(place), device_id_type=MESH)
     for load in loads[4:]:
         load.start()
 
@@ -422,6 +422,7 @@
         lax.fori_loop(0, WIN // GROUP_BATCH, part, 0)
         return carry
 
+    pl.semaphore_wait(plane_sem, WIN - 1)
     lax.fori_loop(0, batch, sample, 0)
 
     out_row = iota((256, 256), 0)
@@ -606,6 +607,7 @@
             dma((samples,)),
             dma((samples,)),
             dma,
+            pltpu.SemaphoreType.REGULAR,
         ],
         compiler_params=pltpu.CompilerParams(
             collective_id=0, has_side_effects=True, vmem_limit_bytes=56 * 2**20

time: 79.8 us -> 78.7 us (0.986)
  Pallas kernels: 79.7 us -> 78.6 us
    pallas_call x1, Pallas kernels: 77.3 us -> 76.2 us  [on_device(): pl.pallas_call(block_kernel, out_shape=jax.ShapeDtypeStruct(tiles.shape,...]
where the time goes in v3:
time: 78.7 us; the launch traced here: 78.6 us
  Pallas kernels  78.6 us (100%)
    pallas_call x1, Pallas kernels, on_device(): pl.pallas_call(block_kernel, out_shape=jax.ShapeDtypeStruct(tiles.shape,...  76.2 us
    pallas_call x1, Pallas kernels, on_device(): pl.pallas_call(copy_kernel, out_shape=jax.ShapeDtypeStruct(tiles.shape, F...  2.39 us

profile of v3, /device:TPU:5, one launch (start us, length us, event | category | flops | bytes accessed | tf_op | source)
XLA Modules:
  0.0 78.6 jit_solution(7617970688050772205)
XLA Ops:
  0.0 76.2 %shard_map.118.source_ref = f32[2,8,8,8,512]{4,3,2,1,0:T(8,128)} custom-call(f32[2,8,8,8,512]{4,3,2,1,0:T(8,128)} %bitcast.5, bf16[2,4,32,256]{3,2,1,0:T(8,128)(2,1)} %context_ref.1, bf16[3,3,256,512]{3,2,1,0:T(8,128)(2,1)} %conv_hbm.1, bf16[512,1536]{1,0:T(8,128)(2,1)} %window_qkv_hbm.1, bf16[512,512]{1,0:T(8,128)(2,1)} %window_out_hbm.1, ...), custom_call_target="tpu_custom_call" | custom-call | flops 10000000000 | bytes 16000000 | tf_op jit(solution)/shard_map/pallas_call | solution.py:570
  76.2 2.4 %shard_map.119 = f32[2,8,8,8,512]{4,3,2,1,0:T(8,128)} custom-call(f32[2,8,8,8,512]{4,3,2,1,0:T(8,128)} %shard_map.118.source_ref), custom_call_target="tpu_custom_call" | custom-call | tf_op jit(solution)/shard_map/pallas_call | solution.py:632

commit v4 on v3

--- a/solution.py
+++ b/solution.py
@@ -386,6 +386,11 @@
         heads = attend(normed, window_qkv, value_t, bias, 0)
         after = before + dot_nn(heads, window_out[...])
         normed = layer_norm(after).reshape(per_part, WIN, WIN, width)
+
+        @pl.when((b == 0) & (part == 0))
+        def _():
+            pl.semaphore_wait(plane_sem, WIN - 1)
+
         for i, place in enumerate(places):
             sent[b, place] = jnp.concatenate(
                 [normed[i, :, :, : width // 2], normed[i, :, :, width // 2 :]], axis=1
@@ -422,7 +427,6 @@
         lax.fori_loop(0, WIN // GROUP_BATCH, part, 0)
         return carry
 
-    pl.semaphore_wait(plane_sem, WIN - 1)
     lax.fori_loop(0, batch, sample, 0)
 
     out_row = iota((256, 256), 0)

time: 78.7 us -> 78.7 us (level)
  no operation moved by 1% of the time
where the time goes in v4:
time: 78.7 us; the launch traced here: 78.6 us
  Pallas kernels  78.6 us (100%)
    pallas_call x1, Pallas kernels, on_device(): pl.pallas_call(block_kernel, out_shape=jax.ShapeDtypeStruct(tiles.shape,...  76.2 us
    pallas_call x1, Pallas kernels, on_device(): pl.pallas_call(copy_kernel, out_shape=jax.ShapeDtypeStruct(tiles.shape, F...  2.39 us

profile of v4, /device:TPU:5, one launch (start us, length us, event | category | flops | bytes accessed | tf_op | source)
XLA Modules:
  0.0 78.6 jit_solution(3445695324618531752)
XLA Ops:
  0.0 76.2 %shard_map.118.source_ref = f32[2,8,8,8,512]{4,3,2,1,0:T(8,128)} custom-call(f32[2,8,8,8,512]{4,3,2,1,0:T(8,128)} %bitcast.5, bf16[2,4,32,256]{3,2,1,0:T(8,128)(2,1)} %context_ref.1, bf16[3,3,256,512]{3,2,1,0:T(8,128)(2,1)} %conv_hbm.1, bf16[512,1536]{1,0:T(8,128)(2,1)} %window_qkv_hbm.1, bf16[512,512]{1,0:T(8,128)(2,1)} %window_out_hbm.1, ...), custom_call_target="tpu_custom_call" | custom-call | flops 10000000000 | bytes 16000000 | tf_op jit(solution)/shard_map/pallas_call | solution.py:574
  76.2 2.4 %shard_map.119 = f32[2,8,8,8,512]{4,3,2,1,0:T(8,128)} custom-call(f32[2,8,8,8,512]{4,3,2,1,0:T(8,128)} %shard_map.118.source_ref), custom_call_target="tpu_custom_call" | custom-call | tf_op jit(solution)/shard_map/pallas_call | solution.py:636
